TPU v7x, 32 devices: a whole 2x2x4 slice. The times are simulated.
32 devices in a mesh: inst: 2 (over y), row: 2 (over x), col: 4 (over z), sub: 2 (over core).
Axes of the slice: x: 2, y: 2, z: 4, core: 2. Of those that a mesh axis runs over, the one named last changes fastest.
Arguments:
- a_blocks: bfloat16 [4, 8, 192, 128, 128], P(('inst', 'row'), ('col', 'sub')), parts along dimension 0, may hold values from -0.02734375 to 0.02734375
- block_rows: int32 [4, 8, 192], P(('inst', 'row'), ('col', 'sub')), parts along dimension 0, may hold values from 0 to 31, as said below
- block_cols: int32 [4, 8, 192], P(('inst', 'row'), ('col', 'sub')), parts along dimension 0, may hold values from 0 to 31
- block_count: int32 [4, 8], P(('inst', 'row'), ('col', 'sub')), parts along dimension 0, may hold values from 24 to 192, as said below
- cost: float32 [65536], P(('inst', 'row', 'col', 'sub')), parts along dimension 0, may hold values from -11 to 11
- lower: float32 [65536], P(('inst', 'row', 'col', 'sub')), parts along dimension 0, may hold values from -1 to 0
- span: float32 [65536], P(('inst', 'row', 'col', 'sub')), parts along dimension 0, may hold values from 0.5 to 4
- bound_kind: int32 [65536], P(('inst', 'row', 'col', 'sub')), parts along dimension 0, may hold values from 0 to 2
- demand: float32 [16, 16384], P(None, ('inst', 'row', 'col', 'sub')), parts along dimension 1, may hold values from -11 to 11
- restart_flags: int32 [8], replicated, may hold values from 0 to 1, as said below
Outputs:
- primal: float32 [16, 65536], P(None, ('inst', 'row', 'col', 'sub')), parts along dimension 1
- dual: float32 [16, 16384], P(None, ('inst', 'row', 'col', 'sub')), parts along dimension 1
There are 2 independent parts, one for each index of `inst`. A program takes and returns all parts, laid end to end along the dimension named above; an argument that names none is the same for every part. Nothing has to cross between parts.
Inputs may be any that keep to these rules, and one draw needn't show every extreme that they name: Within each tile the 192 slots name distinct pairs of block_rows and block_cols. `block_count`: some tile of every part has exactly 192 live slots. `restart_flags`: some iteration in the first half of the 8 iterations restarts; the last iteration never does.
All inputs are finite; a program needn't handle non-finite values.
Results may differ from a plain program's by a relative error of at most 0.0007.
Values may be sent and summed in bfloat16 or wider, within the bound.
A program may use at most 64 MiB of HBM per device.

v0:
```python
import jax
import jax.numpy as jnp
from jax import lax
from jax.sharding import PartitionSpec as P

step_scale = 0.8
tiny = 1e-06


def clamp_box(values, low_side, high_side):
    return jnp.minimum(jnp.maximum(values, low_side), high_side)


def block_apply(vector, blocks, picks, placing, form, count_out):
    scenarios = vector.shape[0]
    width = blocks.shape[-1]
    pieces = vector.reshape(scenarios, -1, width)
    taken = jnp.take(pieces, picks, axis=1)
    products = jnp.einsum(form, taken, blocks, preferred_element_type=jnp.float32)
    summed = jnp.einsum("skb,kg->sgb", products, placing, precision=lax.Precision.HIGHEST)
    return summed.reshape(scenarios, count_out * width)


def shards(
    a_blocks,
    block_rows,
    block_cols,
    block_count,
    cost,
    lower,
    span,
    bound_kind,
    demand,
    restart_flags,
):
    row_devices = lax.axis_size("row")
    col_devices = lax.axis_size(("col", "sub"))
    blocks = a_blocks[0, 0]
    slots = blocks.shape[0]
    width = blocks.shape[-1]
    scenarios = demand.shape[0]
    own_rows = demand.shape[1]
    own_cols = cost.shape[0]
    group_row_blocks = own_rows // width * col_devices
    group_col_blocks = own_cols // width * row_devices
    total_rows = own_rows * row_devices * col_devices
    total_cols = own_cols * row_devices * col_devices
    row_list = block_rows[0, 0]
    col_list = block_cols[0, 0]
    live = jnp.arange(slots) < block_count[0, 0]
    row_place = (
        live[:, None] & (row_list[:, None] == jnp.arange(group_row_blocks)[None, :])
    ).astype(jnp.float32)
    col_place = (
        live[:, None] & (col_list[:, None] == jnp.arange(group_col_blocks)[None, :])
    ).astype(jnp.float32)
    low_own = jnp.where(bound_kind == 2, -1e30, lower)
    high_own = jnp.where(bound_kind == 1, lower + span, 1e30)
    cost_here, low_here, high_here = (
        lax.all_gather(cost, "row", axis=0, tiled=True),
        lax.all_gather(low_own, "row", axis=0, tiled=True),
        lax.all_gather(high_own, "row", axis=0, tiled=True),
    )
    primal_offset = lax.axis_index("row") * own_cols
    primal_length = own_cols * row_devices
    primal = jnp.zeros((scenarios, primal_length), jnp.float32)
    dual = jnp.zeros((scenarios, own_rows), jnp.float32)
    primal_anchor = primal
    dual_anchor = dual
    primal_total = primal
    dual_total = dual
    count = jnp.zeros((), jnp.float32)
    weight = jnp.ones((scenarios, 1), jnp.float32)
    for step in range(restart_flags.shape[0]):
        dual_half = dual.astype(jnp.bfloat16)
        dual_group = lax.all_gather(dual_half, ("col", "sub"), axis=1, tiled=True)
        adjoint_part = block_apply(
            dual_group, blocks, row_list, col_place, "ska,kab->skb", group_col_blocks
        )
        gradient = lax.psum(adjoint_part, "row")
        primal_new = clamp_box(
            primal - step_scale / weight * (cost_here[None, :] - gradient),
            low_here[None, :],
            high_here[None, :],
        )
        primal_bar = (2.0 * primal_new - primal).astype(jnp.bfloat16)
        forward_part = block_apply(
            primal_bar, blocks, col_list, row_place, "skb,kab->ska", group_row_blocks
        )
        image = lax.psum_scatter(forward_part, ("col", "sub"), scatter_dimension=1, tiled=True)
        dual_new = jnp.maximum(dual + step_scale * weight * (demand - image), 0.0)
        primal_total = primal_total + primal_new
        dual_total = dual_total + dual_new
        count = count + 1.0
        primal_mean = primal_total / count
        dual_mean = dual_total / count
        primal_gap = lax.dynamic_slice_in_dim(
            primal_mean - primal_anchor, primal_offset, own_cols, 1
        )
        dual_gap = dual_mean - dual_anchor
        gap_primal, gap_dual = lax.psum(
            (jnp.sum(primal_gap * primal_gap, axis=1), jnp.sum(dual_gap * dual_gap, axis=1)),
            ("row", "col", "sub"),
        )
        ratio = jnp.sqrt((gap_dual / total_rows + tiny) / (gap_primal / total_cols + tiny))
        restart = restart_flags[step] == 1
        weight = jnp.where(restart, jnp.sqrt(weight * ratio[:, None]), weight)
        primal = jnp.where(restart, primal_mean, primal_new)
        dual = jnp.where(restart, dual_mean, dual_new)
        primal_anchor = jnp.where(restart, primal_mean, primal_anchor)
        dual_anchor = jnp.where(restart, dual_mean, dual_anchor)
        primal_total = jnp.where(restart, 0.0, primal_total)
        dual_total = jnp.where(restart, 0.0, dual_total)
        count = jnp.where(restart, 0.0, count)
    primal_own = lax.dynamic_slice_in_dim(primal, primal_offset, own_cols, 1)
    return (primal_own, dual)


def solution(mesh):
    placed = (
        P(("inst", "row"), ("col", "sub"), None, None, None),
        P(("inst", "row"), ("col", "sub"), None),
        P(("inst", "row"), ("col", "sub"), None),
        P(("inst", "row"), ("col", "sub")),
        P(("inst", "row", "col", "sub")),
        P(("inst", "row", "col", "sub")),
        P(("inst", "row", "col", "sub")),
        P(("inst", "row", "col", "sub")),
        P(None, ("inst", "row", "col", "sub")),
        P(),
    )
    return jax.shard_map(
        shards,
        mesh=mesh,
        in_specs=placed,
        out_specs=(P(None, ("inst", "row", "col", "sub")), P(None, ("inst", "row", "col", "sub"))),
        check_vma=False,
    )
```

profile of v0, /device:TPU:0, one launch (start us, length us, event | category | flops | bytes accessed | tf_op | source)
XLA Modules:
  0.0 719.7 jit_solution(1570508812989128147)
XLA Ops:
  16.8 5.3 all_gather.32
  31.6 10.7 %all-reduce.16.cloned.1.call-done = f32[16,4096]{1,0:T(8,128)} async-done(((f32[16,4096]{1,0:T(8,128)}), f32[16,4096]{1,0:T(8,128)}) %all-reduce.16.cloned.1.call-update) | async-done | bytes 262160 | tf_op jit(solution)/shard_map/psum | solution.py:80
  44.1 5.5 fusion.67
  51.7 30.4 %reduce-scatter.9.cloned.1.call-done = f32[16,512]{1,0:T(8,128)} async-done(((f32[16,4096]{1,0:T(8,128)}), f32[16,512]{1,0:T(8,128)}) %reduce-scatter.9.cloned.1.call-update) | async-done | bytes 32784 | tf_op jit(solution)/shard_map/reduce_scatter | solution.py:90
  83.0 14.0 %all_gather.34 = bf16[16,4096]{1,0:T(8,128)(2,1)S(1)} all-gather(bf16[16,512]{1,0:T(8,128)(2,1)S(1)} %convert_element_type.49), channel_id=1, replica_groups=mesh['inst'=2,'row'=2,'col'=4,'sub'=2] {'col','sub'}, dimensions={1}, use_global_device_ids=true | all-gather | bytes 147456 | tf_op jit(solution)/shard_map/all_gather | solution.py:76
  103.7 31.1 %all-reduce.6 = (f32[16]{0:T(128)S(1)}, f32[16]{0:T(128)S(1)}) all-reduce(f32[16]{0:T(128)S(1)} %multiply_reduce_fusion.1, f32[16]{0:T(128)S(1)} %get-tuple-element.69), channel_id=1, replica_groups=mesh['inst'=2,'row'=2,'col'=4,'sub'=2] {'row','col','sub'}, use_global_device_ids=true, to_apply=%region_5.7 | all-reduce | flops 32 | bytes 256 | tf_op jit(solution)/shard_map/psum | solution.py:101
  136.7 5.5 fusion.73
  145.7 26.5 %reduce-scatter.11.cloned.1.call-done = f32[16,512]{1,0:T(8,128)} async-done(((f32[16,4096]{1,0:T(8,128)}), f32[16,512]{1,0:T(8,128)}) %reduce-scatter.11.cloned.1.call-update) | async-done | bytes 32784 | tf_op jit(solution)/shard_map/reduce_scatter | solution.py:90
  173.2 14.0 %all_gather.35 = bf16[16,4096]{1,0:T(8,128)(2,1)S(1)} all-gather(bf16[16,512]{1,0:T(8,128)(2,1)S(1)} %fusion.207), channel_id=1, replica_groups=mesh['inst'=2,'row'=2,'col'=4,'sub'=2] {'col','sub'}, dimensions={1}, use_global_device_ids=true | all-gather | bytes 147456 | tf_op jit(solution)/shard_map/all_gather | solution.py:76
  193.9 30.4 %all-reduce.5 = (f32[16]{0:T(128)S(1)}, f32[16]{0:T(128)S(1)}) all-reduce(f32[16]{0:T(128)S(1)} %fusion.196, f32[16]{0:T(128)S(1)} %get-tuple-element.63), channel_id=1, replica_groups=mesh['inst'=2,'row'=2,'col'=4,'sub'=2] {'row','col','sub'}, use_global_device_ids=true, to_apply=%region_11.13 | all-reduce | flops 32 | bytes 256 | tf_op jit(solution)/shard_map/psum | solution.py:101
  226.5 5.5 fusion.79
  234.2 28.0 %reduce-scatter.13.cloned.1.call-done = f32[16,512]{1,0:T(8,128)} async-done(((f32[16,4096]{1,0:T(8,128)}), f32[16,512]{1,0:T(8,128)}) %reduce-scatter.13.cloned.1.call-update) | async-done | bytes 32784 | tf_op jit(solution)/shard_map/reduce_scatter | solution.py:90
  263.1 14.1 %all_gather.36 = bf16[16,4096]{1,0:T(8,128)(2,1)S(1)} all-gather(bf16[16,512]{1,0:T(8,128)(2,1)S(1)} %fusion.203), channel_id=1, replica_groups=mesh['inst'=2,'row'=2,'col'=4,'sub'=2] {'col','sub'}, dimensions={1}, use_global_device_ids=true | all-gather | bytes 147456 | tf_op jit(solution)/shard_map/all_gather | solution.py:76
  283.9 30.6 %all-reduce.4 = (f32[16]{0:T(128)S(1)}, f32[16]{0:T(128)S(1)}) all-reduce(f32[16]{0:T(128)S(1)} %fusion.194, f32[16]{0:T(128)S(1)} %get-tuple-element.57), channel_id=1, replica_groups=mesh['inst'=2,'row'=2,'col'=4,'sub'=2] {'row','col','sub'}, use_global_device_ids=true, to_apply=%region_17.19 | all-reduce | flops 32 | bytes 256 | tf_op jit(solution)/shard_map/psum | solution.py:101
  316.5 5.5 fusion.85
  325.4 26.5 %reduce-scatter.15.cloned.1.call-done = f32[16,512]{1,0:T(8,128)} async-done(((f32[16,4096]{1,0:T(8,128)}), f32[16,512]{1,0:T(8,128)}) %reduce-scatter.15.cloned.1.call-update) | async-done | bytes 32784 | tf_op jit(solution)/shard_map/reduce_scatter | solution.py:90
  352.9 14.0 %all_gather.37 = bf16[16,4096]{1,0:T(8,128)(2,1)S(1)} all-gather(bf16[16,512]{1,0:T(8,128)(2,1)S(1)} %fusion.204), channel_id=1, replica_groups=mesh['inst'=2,'row'=2,'col'=4,'sub'=2] {'col','sub'}, dimensions={1}, use_global_device_ids=true | all-gather | bytes 147456 | tf_op jit(solution)/shard_map/all_gather | solution.py:76
  373.6 30.7 %all-reduce.3 = (f32[16]{0:T(128)S(1)}, f32[16]{0:T(128)S(1)}) all-reduce(f32[16]{0:T(128)S(1)} %fusion.192, f32[16]{0:T(128)S(1)} %get-tuple-element.46), channel_id=1, replica_groups=mesh['inst'=2,'row'=2,'col'=4,'sub'=2] {'row','col','sub'}, use_global_device_ids=true, to_apply=%region_23.25 | all-reduce | flops 32 | bytes 256 | tf_op jit(solution)/shard_map/psum | solution.py:101
  406.3 5.5 fusion.91
  414.0 27.8 %reduce-scatter.17.cloned.1.call-done = f32[16,512]{1,0:T(8,128)} async-done(((f32[16,4096]{1,0:T(8,128)}), f32[16,512]{1,0:T(8,128)}) %reduce-scatter.17.cloned.1.call-update) | async-done | bytes 32784 | tf_op jit(solution)/shard_map/reduce_scatter | solution.py:90
  442.7 14.0 %all_gather.38 = bf16[16,4096]{1,0:T(8,128)(2,1)S(1)} all-gather(bf16[16,512]{1,0:T(8,128)(2,1)S(1)} %fusion.205), channel_id=1, replica_groups=mesh['inst'=2,'row'=2,'col'=4,'sub'=2] {'col','sub'}, dimensions={1}, use_global_device_ids=true | all-gather | bytes 147456 | tf_op jit(solution)/shard_map/all_gather | solution.py:76
  463.4 30.4 %all-reduce.2 = (f32[16]{0:T(128)S(1)}, f32[16]{0:T(128)S(1)}) all-reduce(f32[16]{0:T(128)S(1)} %fusion.190, f32[16]{0:T(128)S(1)} %get-tuple-element.40), channel_id=1, replica_groups=mesh['inst'=2,'row'=2,'col'=4,'sub'=2] {'row','col','sub'}, use_global_device_ids=true, to_apply=%region_29.31 | all-reduce | flops 32 | bytes 256 | tf_op jit(solution)/shard_map/psum | solution.py:101
  495.8 5.5 fusion.97
  504.0 27.4 %reduce-scatter.19.cloned.1.call-done = f32[16,512]{1,0:T(8,128)} async-done(((f32[16,4096]{1,0:T(8,128)}), f32[16,512]{1,0:T(8,128)}) %reduce-scatter.19.cloned.1.call-update) | async-done | bytes 32784 | tf_op jit(solution)/shard_map/reduce_scatter | solution.py:90
  532.3 14.2 %all_gather.39 = bf16[16,4096]{1,0:T(8,128)(2,1)S(1)} all-gather(bf16[16,512]{1,0:T(8,128)(2,1)S(1)} %fusion.206), channel_id=1, replica_groups=mesh['inst'=2,'row'=2,'col'=4,'sub'=2] {'col','sub'}, dimensions={1}, use_global_device_ids=true | all-gather | bytes 147456 | tf_op jit(solution)/shard_map/all_gather | solution.py:76
  553.3 30.4 %all-reduce.1 = (f32[16]{0:T(128)S(1)}, f32[16]{0:T(128)S(1)}) all-reduce(f32[16]{0:T(128)S(1)} %multiply_reduce_fusion, f32[16]{0:T(128)S(1)} %get-tuple-element.29), channel_id=1, replica_groups=mesh['inst'=2,'row'=2,'col'=4,'sub'=2] {'row','col','sub'}, use_global_device_ids=true, to_apply=%region_35.37 | all-reduce | flops 32 | bytes 256 | tf_op jit(solution)/shard_map/psum | solution.py:101
  585.7 5.5 fusion.103
  593.9 27.3 %reduce-scatter.21.cloned.1.call-done = f32[16,512]{1,0:T(8,128)} async-done(((f32[16,4096]{1,0:T(8,128)}), f32[16,512]{1,0:T(8,128)}) %reduce-scatter.21.cloned.1.call-update) | async-done | bytes 32784 | tf_op jit(solution)/shard_map/reduce_scatter | solution.py:90
  622.2 14.0 %all_gather.40 = bf16[16,4096]{1,0:T(8,128)(2,1)S(1)} all-gather(bf16[16,512]{1,0:T(8,128)(2,1)S(1)} %fusion.202), channel_id=1, replica_groups=mesh['inst'=2,'row'=2,'col'=4,'sub'=2] {'col','sub'}, dimensions={1}, use_global_device_ids=true | all-gather | bytes 147456 | tf_op jit(solution)/shard_map/all_gather | solution.py:76
  642.9 30.8 %all-reduce = (f32[16]{0:T(128)S(1)}, f32[16]{0:T(128)S(1)}) all-reduce(f32[16]{0:T(128)S(1)} %fusion.188, f32[16]{0:T(128)S(1)} %get-tuple-element.21), channel_id=1, replica_groups=mesh['inst'=2,'row'=2,'col'=4,'sub'=2] {'row','col','sub'}, use_global_device_ids=true, to_apply=%region_41.43 | all-reduce | flops 32 | bytes 256 | tf_op jit(solution)/shard_map/psum | solution.py:101
  675.7 5.5 fusion.109
  684.5 26.8 %reduce-scatter.23.cloned.1.call-done = f32[16,512]{1,0:T(8,128)} async-done(((f32[16,4096]{1,0:T(8,128)}), f32[16,512]{1,0:T(8,128)}) %reduce-scatter.23.cloned.1.call-update) | async-done | bytes 32784 | tf_op jit(solution)/shard_map/reduce_scatter | solution.py:90
  (184 shorter events, 105.7 us)
Async XLA Ops:
  7.2 35.1 %all-reduce.16.cloned.1.call-start = ((), (), s32[]{:S(2)}) async-start(), calls=%async_computation.8 | async-start | bytes 524288 | tf_op jit(solution)/shard_map/psum | solution.py:80
  10.1 3.9 copy-start.2
  14.0 2.1 copy-start.4
  14.0 2.7 copy-start.5
  14.0 2.7 copy-start.6
  14.0 2.7 copy-start.7
  14.1 12.4 %copy-start.8 = (f32[2048]{0:T(1024)S(1)}, f32[2048]{0:T(1024)}, u32[]{:S(2)}) copy-start(f32[2048]{0:T(1024)} %param.16) | copy-start | bytes 24580
  16.0 66.1 %reduce-scatter.9.cloned.1.call-start = ((), (), s32[]{:S(2)}) async-start(), calls=%async_computation.9 | async-start | bytes 294912 | tf_op jit(solution)/shard_map/reduce_scatter | solution.py:90
  44.1 5.5 copy-start.3
  49.6 32.5 %copy-start.1 = (f32[16,512]{1,0:T(8,128)S(1)}, f32[16,512]{1,0:T(8,128)}, u32[]{:S(2)}) copy-start(f32[16,512]{1,0:T(8,128)} %param.20) | copy-start | bytes 98308
  51.5 83.3 %all-reduce.18.cloned.1.call-start = ((), (), s32[]{:S(2)}) async-start(), calls=%async_computation.10 | async-start | bytes 524288 | tf_op jit(solution)/shard_map/psum | solution.py:80
  103.6 68.6 %reduce-scatter.11.cloned.1.call-start = ((), (), s32[]{:S(2)}) async-start(), calls=%async_computation.11 | async-start | bytes 294912 | tf_op jit(solution)/shard_map/reduce_scatter | solution.py:90
  144.2 80.1 %all-reduce.20.cloned.1.call-start = ((), (), s32[]{:S(2)}) async-start(), calls=%async_computation.12 | async-start | bytes 524288 | tf_op jit(solution)/shard_map/psum | solution.py:80
  191.8 32.5 %copy-start = (f32[16,4096]{1,0:T(8,128)S(1)}, f32[16,4096]{1,0:T(8,128)}, u32[]{:S(2)}) copy-start(f32[16,4096]{1,0:T(8,128)} %all-reduce.18.cloned.1.call-done) | copy-start | bytes 786436
  193.8 68.3 %reduce-scatter.13.cloned.1.call-start = ((), (), s32[]{:S(2)}) async-start(), calls=%async_computation.13 | async-start | bytes 294912 | tf_op jit(solution)/shard_map/reduce_scatter | solution.py:90
  234.0 80.6 %all-reduce.22.cloned.1.call-start = ((), (), s32[]{:S(2)}) async-start(), calls=%async_computation.14 | async-start | bytes 524288 | tf_op jit(solution)/shard_map/psum | solution.py:80
  283.9 68.0 %reduce-scatter.15.cloned.1.call-start = ((), (), s32[]{:S(2)}) async-start(), calls=%async_computation.15 | async-start | bytes 294912 | tf_op jit(solution)/shard_map/reduce_scatter | solution.py:90
  323.9 80.4 %all-reduce.24.cloned.1.call-start = ((), (), s32[]{:S(2)}) async-start(), calls=%async_computation.16 | async-start | bytes 524288 | tf_op jit(solution)/shard_map/psum | solution.py:80
  373.5 68.2 %reduce-scatter.17.cloned.1.call-start = ((), (), s32[]{:S(2)}) async-start(), calls=%async_computation.17 | async-start | bytes 294912 | tf_op jit(solution)/shard_map/reduce_scatter | solution.py:90
  413.8 80.1 %all-reduce.26.cloned.1.call-start = ((), (), s32[]{:S(2)}) async-start(), calls=%async_computation.18 | async-start | bytes 524288 | tf_op jit(solution)/shard_map/psum | solution.py:80
  463.3 68.1 %reduce-scatter.19.cloned.1.call-start = ((), (), s32[]{:S(2)}) async-start(), calls=%async_computation.19 | async-start | bytes 294912 | tf_op jit(solution)/shard_map/reduce_scatter | solution.py:90
  503.2 80.5 %all-reduce.28.cloned.1.call-start = ((), (), s32[]{:S(2)}) async-start(), calls=%async_computation.20 | async-start | bytes 524288 | tf_op jit(solution)/shard_map/psum | solution.py:80
  553.2 68.0 %reduce-scatter.21.cloned.1.call-start = ((), (), s32[]{:S(2)}) async-start(), calls=%async_computation.21 | async-start | bytes 294912 | tf_op jit(solution)/shard_map/reduce_scatter | solution.py:90
  593.1 80.6 %all-reduce.30.cloned.1.call-start = ((), (), s32[]{:S(2)}) async-start(), calls=%async_computation.22 | async-start | bytes 524288 | tf_op jit(solution)/shard_map/psum | solution.py:80
  642.8 68.4 %reduce-scatter.23.cloned.1.call-start = ((), (), s32[]{:S(2)}) async-start(), calls=%async_computation.23 | async-start | bytes 294912 | tf_op jit(solution)/shard_map/reduce_scatter | solution.py:90
Sparse Core Ops, SparseCore 0:
  16.1 26.0 all-reduce.15
  51.6 30.4 reduce-scatter.8
  103.7 21.3 all-reduce.17
  144.3 27.8 reduce-scatter.10
  193.9 21.3 all-reduce.19
  234.1 27.9 reduce-scatter.12
  284.0 21.3 all-reduce.21
  324.0 27.8 reduce-scatter.14
  373.6 21.3 all-reduce.23
  413.9 27.8 reduce-scatter.16
  463.4 21.3 all-reduce.25
  503.4 27.9 reduce-scatter.18
  553.3 21.3 all-reduce.27
  593.2 27.9 reduce-scatter.20
  643.0 21.3 all-reduce.29
  683.2 27.9 reduce-scatter.22
where the time goes:
time: 727 us; the launch traced here: 720 us
  blocking collectives  327 us (45%)
  waiting for transfers between devices  232 us (32%)
  matrix products  92.1 us (13%)
  local copies, waits for them, and re-layouts  27.1 us (4%)
  between operations  20.9 us (3%)
  other arithmetic  20.5 us (3%)
    reduce_scatter x8, waiting for transfers between devices, shards(): lax.psum_scatter(forward_part, ('col', 'sub'), scatter_dimension=1, tiled...  221 us
    psum x7, blocking collectives, shards(): lax.psum((jnp.sum(primal_gap * primal_gap, axis=1), jnp.sum(dual_gap * du...  214 us
    all_gather x7, blocking collectives, shards(): dual_group = lax.all_gather(dual_half, ('col', 'sub'), axis=1, tiled=True)  98.2 us
    dot_general x16, matrix products, block_apply(): jnp.einsum(form, taken, blocks, preferred_element_type=jnp.float32)  75 us
    dot_general x16, matrix products, block_apply(): jnp.einsum('skb,kg->sgb', products, placing, precision=lax.Precision.HIGH...  17.1 us
  transfers between devices with their start and end apart: 16, of which 9 were waited for; matrix products, arithmetic and copies ran while one was open for 0% of the time, Pallas kernels for 0%

commit v1 on v0

v1 whole, which is shorter than its diff:
```python
import functools

import jax
import jax.numpy as jnp
from jax import lax
from jax.experimental import pallas as pl
from jax.experimental.pallas import tpu as pltpu
from jax.sharding import PartitionSpec as P

step_scale = 0.8
tiny = 1e-06
MESH = pl.DeviceIdType.MESH
BF = jnp.bfloat16
F32 = jnp.float32


def order_slots(key, source, live, groups, dead_source):
    slots = key.shape[0]
    places = jnp.arange(slots, dtype=jnp.int32)
    key = jnp.where(live, key, groups)
    source = jnp.where(live, source, dead_source)
    ahead = (key[None, :] < key[:, None]) | (
        (key[None, :] == key[:, None]) & (places[None, :] < places[:, None])
    )
    rank = jnp.sum(ahead.astype(jnp.int32), axis=1)
    hit = rank[None, :] == places[:, None]
    slot = jnp.sum(jnp.where(hit, places[None, :], 0), axis=1)
    sorted_key = jnp.sum(jnp.where(hit, key[None, :], 0), axis=1)
    sorted_source = jnp.sum(jnp.where(hit, source[None, :], 0), axis=1)
    before = jnp.concatenate([jnp.full((1,), -1, jnp.int32), sorted_key[:-1]])
    same = (before == sorted_key).astype(F32)
    names = jnp.arange(groups, dtype=jnp.int32)
    upto = jnp.sum((key[None, :] <= names[:, None]).astype(jnp.int32), axis=1)
    own = jnp.sum((key[None, :] == names[:, None]).astype(jnp.int32), axis=1)
    last = jnp.where(own > 0, upto - 1, slots)
    return slot, sorted_source, same, last


def kernel(
    sizes,
    index_ref,
    same_ref,
    last_row_ref,
    last_col_ref,
    flags_ref,
    blocks_hbm,
    cost_ref,
    lower_ref,
    span_ref,
    kind_ref,
    demand_ref,
    primal_out,
    dual_out,
    blocks,
    sums,
    bar,
    dual_all,
    bounds,
    primal,
    primal_new,
    primal_anchor,
    primal_total,
    dual,
    dual_anchor,
    dual_total,
    image_send,
    image_recv,
    adjoint_send,
    adjoint_recv,
    gap_all,
    gap_rows,
    weight_ref,
    copy_sem,
    bound_sems,
    dual_sems,
    gap_sems,
    image_sems,
    adjoint_sems,
    gap_row_sems,
):
    rows, cols, subs, iters, slots, own_rb, own_cb, unroll = sizes
    peers = cols * subs
    row_blocks = own_rb * peers
    col_blocks = own_cb * rows
    total_rows = own_rb * 128 * rows * peers
    total_cols = own_cb * 128 * rows * peers
    r = lax.axis_index("row")
    c = lax.axis_index("col") * subs + lax.axis_index("sub")

    load = pltpu.make_async_copy(blocks_hbm, blocks, copy_sem)
    load.start()

    def line(o):
        p = lax.rem(c + o, peers)
        return p, {"col": p // subs, "sub": lax.rem(p, subs)}

    def across(o):
        p = lax.rem(r + o, rows)
        return p, {"row": p}

    barrier = pltpu.get_barrier_semaphore()
    for o in range(1, peers):
        pl.semaphore_signal(barrier, inc=1, device_id=line(o)[1], device_id_type=MESH)
    for o in range(1, rows):
        pl.semaphore_signal(barrier, inc=1, device_id=across(o)[1], device_id_type=MESH)
    pl.semaphore_wait(barrier, peers + rows - 2)

    def push(src, dst, sems, mine, other, device):
        return pltpu.make_async_remote_copy(
            src_ref=src,
            dst_ref=dst,
            send_sem=sems.at[0, other],
            recv_sem=sems.at[1, mine],
            device_id=device,
            device_id_type=MESH,
        )

    kind = kind_ref[...]
    bounds[r, 0] = cost_ref[...]
    bounds[r, 1] = jnp.where(kind == 2, -1e30, lower_ref[...])
    bounds[r, 2] = jnp.where(kind == 1, lower_ref[...] + span_ref[...], 1e30)

    def bound_copy(o, dst):
        p, device = across(o)
        return push(bounds.at[r], bounds.at[dst(p)], bound_sems, dst(p), p, device)

    for o in range(1, rows):
        bound_copy(o, lambda p: r).start()
    zero = jnp.zeros((16, 128), F32)
    sums[slots] = zero
    bar[col_blocks] = zero.astype(BF)
    dual_all[row_blocks] = zero.astype(BF)
    weight_ref[...] = jnp.ones((16, 128), F32)
    dual[...] = jnp.zeros_like(dual)
    dual_anchor[...] = jnp.zeros_like(dual)
    dual_total[...] = jnp.zeros_like(dual)
    for o in range(1, rows):
        bound_copy(o, lambda p: p).wait_recv()
    for o in range(1, rows):
        bound_copy(o, lambda p: r).wait_send()

    for q in range(rows):
        for i in range(own_cb):
            j = q * own_cb + i
            new = -step_scale * bounds[q, 0, i : i + 1, :]
            new = jnp.minimum(
                jnp.maximum(new, bounds[q, 1, i : i + 1, :]), bounds[q, 2, i : i + 1, :]
            )
            new = jnp.broadcast_to(new, (16, 128))
            primal_new[j] = new
            bar[j] = (2.0 * new).astype(BF)
            primal[j] = zero
            primal_anchor[j] = zero
            primal_total[j] = zero
    load.wait()

    def product(source, which, contract):
        def body(i, acc):
            for u in range(unroll):
                k = i * unroll + u
                part = lax.dot_general(
                    source[index_ref[2 * which + 1, k]],
                    blocks[index_ref[2 * which, k]],
                    (((1,), (contract,)), ((), ())),
                    preferred_element_type=F32,
                )
                acc = acc * same_ref[which, k] + part
                sums[k] = acc
            return acc

        lax.fori_loop(0, slots // unroll, body, zero)

    def iteration(t, count):
        restart = flags_ref[t] == 1
        count = count + 1.0
        share = 1.0 / jnp.full((16, 128), count, F32)

        product(bar, 0, 1)

        def image_copy(o, dst):
            p, device = line(o)
            return push(
                image_send.at[p], image_recv.at[dst(p)], image_sems, dst(p), p, device
            )

        for o in range(1, peers):
            p, device = line(o)
            for i in range(own_rb):
                image_send[p, i] = sums[last_row_ref[p * own_rb + i]].astype(BF)
            image_copy(o, lambda p: c).start()

        def settle(j, gap):
            new = primal_new[j]
            total = primal_total[j] + new
            mean = total * share
            anchor = primal_anchor[j]
            primal[j] = jnp.where(restart, mean, new)
            primal_anchor[j] = jnp.where(restart, mean, anchor)
            primal_total[j] = jnp.where(restart, 0.0, total)
            away = mean - anchor
            return gap + away * away

        def settle_group(q, unused):
            def four(i, gap):
                for u in range(4):
                    gap = settle(q * own_cb + i * 4 + u, gap)
                return gap

            return lax.fori_loop(0, own_cb // 4, four, zero)

        gap_x = zero
        for o in range(1, rows):
            settle_group(lax.rem(r + o, rows), None)
        gap_x = settle_group(r, None)

        image = [sums[last_row_ref[c * own_rb + i]] for i in range(own_rb)]
        for o in range(1, peers):
            image_copy(o, lambda p: p).wait_recv()
        for o in range(1, peers):
            p, _ = line(o)
            for i in range(own_rb):
                image[i] = image[i] + image_recv[p, i].astype(F32)
        gap_y = zero
        weight = weight_ref[...]
        for i in range(own_rb):
            demand = demand_ref[:, i * 128 : (i + 1) * 128]
            new = jnp.maximum(dual[i] + step_scale * weight * (demand - image[i]), 0.0)
            total = dual_total[i] + new
            mean = total * share
            anchor = dual_anchor[i]
            value = jnp.where(restart, mean, new)
            dual[i] = value
            dual_all[c * own_rb + i] = value.astype(BF)
            dual_anchor[i] = jnp.where(restart, mean, anchor)
            dual_total[i] = jnp.where(restart, 0.0, total)
            away = mean - anchor
            gap_y = gap_y + away * away
        for o in range(1, peers):
            image_copy(o, lambda p: c).wait_send()

        @pl.when(t < iters - 1)
        def _():
            def dual_copy(o, dst):
                p, device = line(o)
                s = dst(p)
                return push(
                    dual_all.at[pl.ds(c * own_rb, own_rb)],
                    dual_all.at[pl.ds(s * own_rb, own_rb)],
                    dual_sems,
                    s,
                    p,
                    device,
                )

            for o in range(1, peers):
                dual_copy(o, lambda p: c).start()

            low = lax.broadcasted_iota(jnp.int32, (16, 128), 1) < 64
            gap_all[c] = jnp.where(
                low,
                gap_x + pltpu.roll(gap_x, 64, 1),
                gap_y + pltpu.roll(gap_y, 64, 1),
            )

            def gap_copy(o, dst):
                p, device = line(o)
                s = dst(p)
                return push(gap_all.at[c], gap_all.at[s], gap_sems, s, p, device)

            for o in range(1, peers):
                gap_copy(o, lambda p: c).start()
            for o in range(1, peers):
                dual_copy(o, lambda p: p).wait_recv()

            product(dual_all, 1, 0)

            slot = lax.rem(t, 2)
            def adjoint_copy(o, dst):
                p, device = across(o)
                s = dst(p)
                return push(
                    adjoint_send,
                    adjoint_recv.at[slot, s],
                    adjoint_sems.at[slot],
                    s,
                    p,
                    device,
                )

            def pack(i, unused):
                for u in range(8):
                    j = i * 8 + u
                    adjoint_send[j] = sums[last_col_ref[j]].astype(BF)
                return unused

            lax.fori_loop(0, col_blocks // 8, pack, 0)
            for o in range(1, rows):
                adjoint_copy(o, lambda p: r).start()

            for o in range(1, peers):
                gap_copy(o, lambda p: p).wait_recv()
            gap = gap_all[0]
            for p in range(1, peers):
                gap = gap + gap_all[p]
            gap_rows[slot, r] = gap

            def gap_row_copy(o, dst):
                p, device = across(o)
                s = dst(p)
                return push(
                    gap_rows.at[slot, r],
                    gap_rows.at[slot, s],
                    gap_row_sems.at[slot],
                    s,
                    p,
                    device,
                )

            for o in range(1, rows):
                gap_row_copy(o, lambda p: r).start()
            for o in range(1, rows):
                gap_row_copy(o, lambda p: p).wait_recv()
            gap = gap_rows[slot, 0]
            for p in range(1, rows):
                gap = gap + gap_rows[slot, p]
            sum_x = jnp.sum(jnp.where(low, gap, 0.0), axis=1, keepdims=True)
            sum_y = jnp.sum(jnp.where(low, 0.0, gap), axis=1, keepdims=True)
            sum_x = jnp.broadcast_to(sum_x, (16, 128))
            sum_y = jnp.broadcast_to(sum_y, (16, 128))
            ratio = jnp.sqrt((sum_y / total_rows + tiny) / (sum_x / total_cols + tiny))
            fresh = jnp.where(restart, jnp.sqrt(weight * ratio), weight)
            weight_ref[...] = fresh
            stride = step_scale / fresh

            for o in range(1, rows):
                adjoint_copy(o, lambda p: p).wait_recv()

            for q in range(rows):

                def update(i, unused):
                    for u in range(4):
                        n = i * 4 + u
                        j = q * own_cb + n
                        gradient = sums[last_col_ref[j]]
                        for o in range(1, rows):
                            p, _ = across(o)
                            gradient = gradient + adjoint_recv[slot, p, j].astype(F32)
                        old = primal[j]
                        new = old - stride * (bounds[q, 0, pl.ds(n, 1), :] - gradient)
                        new = jnp.maximum(new, bounds[q, 1, pl.ds(n, 1), :])
                        new = jnp.minimum(new, bounds[q, 2, pl.ds(n, 1), :])
                        primal_new[j] = new
                        bar[j] = (2.0 * new - old).astype(BF)
                    return unused

                lax.fori_loop(0, own_cb // 4, update, 0)

            for o in range(1, peers):
                dual_copy(o, lambda p: c).wait_send()
                gap_copy(o, lambda p: c).wait_send()
            for o in range(1, rows):
                adjoint_copy(o, lambda p: r).wait_send()
                gap_row_copy(o, lambda p: r).wait_send()

        return jnp.where(restart, 0.0, count)

    lax.fori_loop(0, iters, iteration, jnp.zeros((), F32))
    for i in range(own_cb):
        primal_out[:, i * 128 : (i + 1) * 128] = primal[r * own_cb + i]
    for i in range(own_rb):
        dual_out[:, i * 128 : (i + 1) * 128] = dual[i]


def shards(
    rows,
    cols,
    subs,
    a_blocks,
    block_rows,
    block_cols,
    block_count,
    cost,
    lower,
    span,
    bound_kind,
    demand,
    restart_flags,
):
    blocks = a_blocks[0, 0]
    slots = blocks.shape[0]
    peers = cols * subs
    own_rb = demand.shape[1] // 128
    own_cb = cost.shape[0] // 128
    row_blocks = own_rb * peers
    col_blocks = own_cb * rows
    iters = restart_flags.shape[0]
    unroll = 32 if slots % 32 == 0 else 1
    live = jnp.arange(slots) < block_count[0, 0]
    row_list = block_rows[0, 0]
    col_list = block_cols[0, 0]
    slot_f, source_f, same_f, last_row = order_slots(
        row_list, col_list, live, row_blocks, col_blocks
    )
    slot_a, source_a, same_a, last_col = order_slots(
        col_list, row_list, live, col_blocks, row_blocks
    )
    index = jnp.stack([slot_f, source_f, slot_a, source_a])
    same = jnp.stack([same_f, same_a])
    sizes = (rows, cols, subs, iters, slots, own_rb, own_cb, unroll)
    smem = pl.BlockSpec(memory_space=pltpu.SMEM)
    vmem = pl.BlockSpec(memory_space=pltpu.VMEM)
    dma = pltpu.SemaphoreType.DMA
    tile = (16, 128)
    call = pl.pallas_call(
        functools.partial(kernel, sizes),
        out_shape=(
            jax.ShapeDtypeStruct((16, own_cb * 128), F32),
            jax.ShapeDtypeStruct((16, own_rb * 128), F32),
        ),
        in_specs=[smem] * 5 + [pl.BlockSpec(memory_space=pl.ANY)] + [vmem] * 5,
        out_specs=(vmem, vmem),
        scratch_shapes=[
            pltpu.VMEM((slots, 128, 128), BF),
            pltpu.VMEM((slots + 1,) + tile, F32),
            pltpu.VMEM((col_blocks + 1,) + tile, BF),
            pltpu.VMEM((row_blocks + 1,) + tile, BF),
            pltpu.VMEM((rows, 3, own_cb, 128), F32),
            pltpu.VMEM((col_blocks,) + tile, F32),
            pltpu.VMEM((col_blocks,) + tile, F32),
            pltpu.VMEM((col_blocks,) + tile, F32),
            pltpu.VMEM((col_blocks,) + tile, F32),
            pltpu.VMEM((own_rb,) + tile, F32),
            pltpu.VMEM((own_rb,) + tile, F32),
            pltpu.VMEM((own_rb,) + tile, F32),
            pltpu.VMEM((peers, own_rb) + tile, BF),
            pltpu.VMEM((peers, own_rb) + tile, BF),
            pltpu.VMEM((col_blocks,) + tile, BF),
            pltpu.VMEM((2, rows, col_blocks) + tile, BF),
            pltpu.VMEM((peers,) + tile, F32),
            pltpu.VMEM((2, rows) + tile, F32),
            pltpu.VMEM(tile, F32),
            dma,
            dma((2, rows)),
            dma((2, peers)),
            dma((2, peers)),
            dma((2, peers)),
            dma((2, 2, rows)),
            dma((2, 2, rows)),
        ],
        compiler_params=pltpu.CompilerParams(
            collective_id=0,
            has_side_effects=True,
            vmem_limit_bytes=40 * 1024 * 1024,
        ),
    )
    as_blocks = lambda v: v.reshape(own_cb, 128)
    return call(
        index,
        same,
        last_row,
        last_col,
        restart_flags,
        blocks,
        as_blocks(cost),
        as_blocks(lower),
        as_blocks(span),
        as_blocks(bound_kind),
        demand,
    )


def solution(mesh):
    placed = (
        P(("inst", "row"), ("col", "sub"), None, None, None),
        P(("inst", "row"), ("col", "sub"), None),
        P(("inst", "row"), ("col", "sub"), None),
        P(("inst", "row"), ("col", "sub")),
        P(("inst", "row", "col", "sub")),
        P(("inst", "row", "col", "sub")),
        P(("inst", "row", "col", "sub")),
        P(("inst", "row", "col", "sub")),
        P(None, ("inst", "row", "col", "sub")),
        P(),
    )
    shape = mesh.shape
    return jax.shard_map(
        functools.partial(shards, shape["row"], shape["col"], shape["sub"]),
        mesh=mesh,
        in_specs=placed,
        out_specs=(P(None, ("inst", "row", "col", "sub")), P(None, ("inst", "row", "col", "sub"))),
        check_vma=False,
    )
```

time: 727 us -> 179 us (0.25); the launches traced: 720 us -> 179 us
  blocking collectives: 327 us -> 0 us
  waiting for transfers between devices: 232 us -> 0 us
  Pallas kernels: 0 us -> 168 us
  matrix products: 92.1 us -> 0 us
  between operations: 20.9 us -> 1.33 us
  local copies, waits for them, and re-layouts: 27.1 us -> 8.25 us
  other arithmetic: 20.5 us -> 1.86 us
    reduce_scatter x8 -> x0, waiting for transfers between devices: 221 us -> none  [shards(): lax.psum_scatter(forward_part, ('col', 'sub'), scatter_dimension=1, tiled...]
    psum x7 -> x0, blocking collectives: 214 us -> none  [shards(): lax.psum((jnp.sum(primal_gap * primal_gap, axis=1), jnp.sum(dual_gap * du...]
    pallas_call x0 -> x1, Pallas kernels: none -> 168 us  [shards(): call(index, same, last_row, last_col, restart_flags, blocks, as_blocks(co...]
    all_gather x10 -> x0, blocking collectives: 112 us -> none  [the longest x7 98.2 us: shards(): dual_group = lax.all_gather(dual_half, ('col', 'sub'), axis=1, tiled=True)]
    dot_general x32 -> x0, matrix products: 92.1 us -> none  [the longest x16 75 us: block_apply(): jnp.einsum(form, taken, blocks, preferred_element_type=jnp.float32)]
    gather x16 -> x0, local copies, waits for them, and re-layouts: 12.5 us -> none  [block_apply(): taken = jnp.take(pieces, picks, axis=1)]
    psum x8 -> x0, waiting for transfers between devices: 10.8 us -> none  [shards(): gradient = lax.psum(adjoint_part, 'row')]
  transfers between devices with their start and end apart: 16 -> 0, of which waited for: 9 -> 0; matrix products, arithmetic and copies ran while one was open for 0% -> 0% of each run, Pallas kernels for 0% -> 0%
where the time goes in v1:
time: 179 us
  Pallas kernels  168 us (94%)
  local copies, waits for them, and re-layouts  8.25 us (5%)
  other arithmetic  1.86 us (1%)
    pallas_call x1, Pallas kernels, shards(): call(index, same, last_row, last_col, restart_flags, blocks, as_blocks(co...  168 us
    unnamed x16, local copies, waits for them, and re-layouts  8.25 us

profile of v1, /device:TPU:0, one launch (start us, length us, event | category | flops | bytes accessed | tf_op | source)
XLA Modules:
  0.0 179.1 jit_solution(13539702224107009129)
XLA Ops:
  1.3 0.7 fusion.6
  2.0 0.2 convert_reduce_fusion
  2.2 0.2 convert_reduce_fusion.1
  2.4 0.1 convert_reduce_fusion.2
  2.5 0.1 convert_reduce_fusion.4
  2.6 0.3 select_reduce_fusion.1
  3.0 0.1 fusion.5
  3.1 0.1 fusion.4
  3.2 0.0 copy-start
  3.2 2.8 %copy-done = bf16[1,1,192,128,128]{4,3,2,1,0:T(8,128)(2,1)S(1)} copy-done((bf16[1,1,192,128,128]{4,3,2,1,0:T(8,128)(2,1)S(1)}, bf16[1,1,192,128,128]{4,3,2,1,0:T(8,128)(2,1)}, u32[]{:S(2)}) %copy-start) | copy-done | bytes 6291480
  6.0 0.0 copy-start.1
  6.0 0.8 copy-done.1
  6.7 0.0 copy-start.2
  6.7 0.7 copy-done.2
  7.4 0.0 copy-start.3
  7.4 0.7 copy-done.3
  8.1 0.0 copy-start.4
  8.1 0.7 copy-done.4
  8.8 0.0 copy-start.5
  8.8 0.7 copy-done.5
  9.5 0.0 copy-start.6
  9.5 0.7 copy-done.6
  10.2 167.7 %shard_map.113 = (f32[16,2048]{1,0:T(8,128)S(1)}, f32[16,512]{1,0:T(8,128)S(1)}) custom-call(s32[4,192]{1,0:T(4,128)S(1)} %pad_add_fusion.index_ref, f32[2,192]{1,0:T(2,128)S(1)} %add_convert_fusion.same_ref, s32[32]{0:T(128)S(1)} %compare_select_fusion.1.last_row_ref, s32[32]{0:T(128)S(1)} %compare_select_fusion.last_col_ref, s32[8]{0:T(128)S(1)} %copy-done.6, ...), custom_call_target="tpu_custom_call" | custom-call | tf_op jit(solution)/shard_map/pallas_call | solution.py:457
  177.8 0.7 copy.15
  178.5 0.6 copy.16
  (4 shorter events, 0.0 us)
Async XLA Ops:
  3.2 2.8 %copy-start = (bf16[1,1,192,128,128]{4,3,2,1,0:T(8,128)(2,1)S(1)}, bf16[1,1,192,128,128]{4,3,2,1,0:T(8,128)(2,1)}, u32[]{:S(2)}) copy-start(bf16[1,1,192,128,128]{4,3,2,1,0:T(8,128)(2,1)} %param.10) | copy-start | bytes 18874372
  6.0 0.8 copy-start.1
  6.7 0.7 copy-start.2
  7.4 0.7 copy-start.3
  8.1 0.7 copy-start.4
  8.8 0.7 copy-start.5
  9.5 0.7 copy-start.6

commit v2 on v1

v2 whole, which is shorter than its diff:
```python
import functools

import jax
import jax.numpy as jnp
from jax import lax
from jax.experimental import pallas as pl
from jax.experimental.pallas import tpu as pltpu
from jax.sharding import PartitionSpec as P

step_scale = 0.8
tiny = 1e-06
MESH = pl.DeviceIdType.MESH
BF = jnp.bfloat16
F32 = jnp.float32


def order_slots(key, source, live, groups, dead_source):
    slots = key.shape[0]
    places = jnp.arange(slots, dtype=jnp.int32)
    key = jnp.where(live, key, groups)
    source = jnp.where(live, source, dead_source)
    ahead = (key[None, :] < key[:, None]) | (
        (key[None, :] == key[:, None]) & (places[None, :] < places[:, None])
    )
    rank = jnp.sum(ahead.astype(jnp.int32), axis=1)
    hit = rank[None, :] == places[:, None]
    slot = jnp.sum(jnp.where(hit, places[None, :], 0), axis=1)
    sorted_key = jnp.sum(jnp.where(hit, key[None, :], 0), axis=1)
    sorted_source = jnp.sum(jnp.where(hit, source[None, :], 0), axis=1)
    before = jnp.concatenate([jnp.full((1,), -1, jnp.int32), sorted_key[:-1]])
    same = (before == sorted_key).astype(F32)
    names = jnp.arange(groups, dtype=jnp.int32)
    upto = jnp.sum((key[None, :] <= names[:, None]).astype(jnp.int32), axis=1)
    own = jnp.sum((key[None, :] == names[:, None]).astype(jnp.int32), axis=1)
    last = jnp.where(own > 0, upto - 1, slots)
    return slot, sorted_source, same, last


def kernel(
    sizes,
    index_ref,
    same_ref,
    last_row_ref,
    last_col_ref,
    flags_ref,
    blocks_hbm,
    cost_hbm,
    lower_hbm,
    span_hbm,
    kind_hbm,
    demand_hbm,
    primal_out,
    dual_out,
    blocks,
    flipped,
    vectors,
    kind_ref,
    demand_ref,
    sums,
    bar,
    dual_all,
    bounds,
    primal,
    primal_new,
    primal_anchor,
    primal_total,
    dual,
    dual_anchor,
    dual_total,
    pair_send,
    pair_recv,
    image_send,
    image_recv,
    adjoint_send,
    adjoint_recv,
    gap_line,
    gap_group,
    weight_ref,
    copy_sems,
    bound_sems,
    pair_sems,
    image_sems,
    dual_sems,
    forward_sems,
    gap_sems,
    group_sems,
    adjoint_sems,
):
    rows, cols, subs, iters, slots, own_rb, own_cb, unroll, chunk = sizes
    group = rows * subs
    row_blocks = own_rb * cols * subs
    col_blocks = own_cb * rows
    chunks = col_blocks // chunk
    total_rows = own_rb * 128 * rows * cols * subs
    total_cols = own_cb * 128 * rows * cols * subs
    r = lax.axis_index("row")
    z = lax.axis_index("col")
    s = lax.axis_index("sub")
    g = r * subs + s

    loads = [
        pltpu.make_async_copy(cost_hbm, vectors.at[0], copy_sems.at[0]),
        pltpu.make_async_copy(lower_hbm, vectors.at[1], copy_sems.at[1]),
        pltpu.make_async_copy(span_hbm, vectors.at[2], copy_sems.at[2]),
        pltpu.make_async_copy(kind_hbm, kind_ref, copy_sems.at[3]),
        pltpu.make_async_copy(demand_hbm, demand_ref, copy_sems.at[4]),
        pltpu.make_async_copy(blocks_hbm, blocks, copy_sems.at[5]),
    ]
    for load in loads:
        load.start()

    def along(o):
        if cols & (cols - 1):
            return lax.rem(z + o, cols)
        p = z
        bit = 1
        while bit < cols:
            if o & bit:
                p = p + bit * (1 - 2 * lax.rem(lax.div(z, bit), 2))
            bit *= 2
        return p

    def across(o):
        return lax.rem(r + o, rows)

    def beside(o):
        return lax.rem(s + o, subs)

    def around(o):
        p = lax.rem(g + o, group)
        return p, {"row": lax.div(p, subs), "sub": lax.rem(p, subs)}

    barrier = pltpu.get_barrier_semaphore()
    for o in range(1, cols):
        pl.semaphore_signal(barrier, inc=1, device_id={"col": along(o)}, device_id_type=MESH)
    for o in range(1, group):
        pl.semaphore_signal(barrier, inc=1, device_id=around(o)[1], device_id_type=MESH)
    pl.semaphore_wait(barrier, cols + group - 2)

    def push(src, dst, send_sem, recv_sem, device):
        return pltpu.make_async_remote_copy(
            src_ref=src,
            dst_ref=dst,
            send_sem=send_sem,
            recv_sem=recv_sem,
            device_id=device,
            device_id_type=MESH,
        )

    def bound_copy(o, mine):
        p = across(o)
        n = r if mine else p
        return push(
            bounds.at[r], bounds.at[n], bound_sems.at[0, p], bound_sems.at[1, n], {"row": p}
        )

    def pair_copy(o, q, mine):
        p = beside(o)
        n = s if mine else p
        return push(
            pair_send.at[p, q],
            pair_recv.at[n, q],
            pair_sems.at[0, p, q],
            pair_sems.at[1, n, q],
            {"sub": p},
        )

    def image_copy(o, mine):
        p = along(o)
        n = z if mine else p
        return push(
            image_send.at[p],
            image_recv.at[n],
            image_sems.at[0, p],
            image_sems.at[1, n],
            {"col": p},
        )

    def dual_part(q, n):
        return dual_all.at[pl.ds((q * subs + n) * own_rb, own_rb)]

    def dual_copy(o, mine):
        p = along(o)
        n = z if mine else p
        return push(
            dual_part(z, s), dual_part(n, s), dual_sems.at[0, p], dual_sems.at[1, n], {"col": p}
        )

    def forward_copy(o, q, mine):
        p = beside(o)
        n = s if mine else p
        return push(
            dual_part(q, s),
            dual_part(q, n),
            forward_sems.at[0, p, q],
            forward_sems.at[1, n, q],
            {"sub": p},
        )

    def gap_copy(o, mine):
        p = along(o)
        n = z if mine else p
        return push(
            gap_line.at[z], gap_line.at[n], gap_sems.at[0, p], gap_sems.at[1, n], {"col": p}
        )

    def group_copy(o, slot, mine):
        p, device = around(o)
        n = g if mine else p
        return push(
            gap_group.at[slot, g],
            gap_group.at[slot, n],
            group_sems.at[slot, 0, p],
            group_sems.at[slot, 1, n],
            device,
        )

    def adjoint_copy(o, slot, part, mine):
        p = across(o)
        n = r if mine else p
        span = pl.ds(part * chunk, chunk)
        return push(
            adjoint_send.at[span],
            adjoint_recv.at[slot, n, span],
            adjoint_sems.at[slot, 0, p, part],
            adjoint_sems.at[slot, 1, n, part],
            {"row": p},
        )

    for load in loads[:4]:
        load.wait()
    kind = kind_ref[...]
    bounds[r, 0] = vectors[0]
    bounds[r, 1] = jnp.where(kind == 2, -1e30, vectors[1])
    bounds[r, 2] = jnp.where(kind == 1, vectors[1] + vectors[2], 1e30)
    for o in range(1, rows):
        bound_copy(o, True).start()
    zero = jnp.zeros((16, 128), F32)
    none = jnp.zeros((16, 128), BF)
    sums[slots] = zero
    bar[col_blocks] = none
    dual_all[row_blocks] = none
    weight_ref[...] = jnp.ones((16, 128), F32)
    dual[...] = jnp.zeros_like(dual)
    dual_anchor[...] = jnp.zeros_like(dual)
    dual_total[...] = jnp.zeros_like(dual)
    loads[4].wait()
    loads[5].wait()

    def flip(i, unused):
        for u in range(16):
            k = i * 16 + u
            flipped[k] = blocks[index_ref[0, k]].T
        return unused

    lax.fori_loop(0, slots // 16, flip, 0)

    for o in range(1, rows):
        bound_copy(o, False).wait_recv()
    for o in range(1, rows):
        bound_copy(o, True).wait_send()

    for q in range(rows):
        for i in range(own_cb):
            j = q * own_cb + i
            new = -step_scale * bounds[q, 0, i : i + 1, :]
            new = jnp.minimum(
                jnp.maximum(new, bounds[q, 1, i : i + 1, :]), bounds[q, 2, i : i + 1, :]
            )
            new = jnp.broadcast_to(new, (16, 128))
            primal_new[j] = new
            bar[j] = (2.0 * new).astype(BF)
            primal[j] = zero
            primal_anchor[j] = zero
            primal_total[j] = zero

    def product(source, which, pair_of):
        def body(i, acc):
            for u in range(0, unroll, 2):
                k = i * unroll + u
                first = source[index_ref[2 * which + 1, k]]
                second = source[index_ref[2 * which + 1, k + 1]]
                left = jnp.concatenate(
                    [
                        jnp.concatenate([first, none], 1),
                        jnp.concatenate([none, second], 1),
                    ],
                    0,
                )
                parts = jnp.dot(left, pair_of(k), preferred_element_type=F32)
                acc = acc * same_ref[which, k] + parts[:16]
                sums[k] = acc
                acc = acc * same_ref[which, k + 1] + parts[16:]
                sums[k + 1] = acc
            return acc

        lax.fori_loop(0, slots // unroll, body, zero)

    def forward_pair(k):
        return jnp.concatenate([flipped[k], flipped[k + 1]], 0)

    def adjoint_pair(k):
        return jnp.concatenate([blocks[index_ref[2, k]], blocks[index_ref[2, k + 1]]], 0)

    def iteration(t, count):
        restart = flags_ref[t] == 1
        slot = lax.rem(t, 2)
        count = count + 1.0
        share = 1.0 / jnp.full((16, 128), count, F32)

        product(bar, 0, forward_pair)
        order = [along(o) for o in range(cols - 1, 0, -1)] + [z]
        for q in order:
            for o in range(1, subs):
                p = beside(o)
                for i in range(own_rb):
                    pair_send[p, q, i] = sums[last_row_ref[(q * subs + p) * own_rb + i]]
                pair_copy(o, q, True).start()

        def pair_sum(q):
            for o in range(1, subs):
                pair_copy(o, q, False).wait_recv()
            total = []
            for i in range(own_rb):
                value = sums[last_row_ref[(q * subs + s) * own_rb + i]]
                for o in range(1, subs):
                    value = value + pair_recv[beside(o), q, i]
                total.append(value)
            return total

        for o in range(cols - 1, 0, -1):
            q = along(o)
            total = pair_sum(q)
            for i in range(own_rb):
                image_send[q, i] = total[i].astype(BF)
            image_copy(o, True).start()
        image = pair_sum(z)

        def settle(j, gap):
            new = primal_new[j]
            total = primal_total[j] + new
            mean = total * share
            anchor = primal_anchor[j]
            primal[j] = jnp.where(restart, mean, new)
            primal_anchor[j] = jnp.where(restart, mean, anchor)
            primal_total[j] = jnp.where(restart, 0.0, total)
            away = mean - anchor
            return gap + away * away

        def settle_group(q):
            def four(i, gap):
                for u in range(4):
                    gap = settle(q * own_cb + i * 4 + u, gap)
                return gap

            return lax.fori_loop(0, own_cb // 4, four, zero)

        for o in range(1, rows):
            settle_group(across(o))
        gap_x = settle_group(r)

        for o in range(1, cols):
            image_copy(o, False).wait_recv()
            for i in range(own_rb):
                image[i] = image[i] + image_recv[along(o), i].astype(F32)
        gap_y = zero
        weight = weight_ref[...]
        for i in range(own_rb):
            demand = demand_ref[:, i * 128 : (i + 1) * 128]
            new = jnp.maximum(dual[i] + step_scale * weight * (demand - image[i]), 0.0)
            total = dual_total[i] + new
            mean = total * share
            anchor = dual_anchor[i]
            value = jnp.where(restart, mean, new)
            dual[i] = value
            dual_all[(z * subs + s) * own_rb + i] = value.astype(BF)
            dual_anchor[i] = jnp.where(restart, mean, anchor)
            dual_total[i] = jnp.where(restart, 0.0, total)
            away = mean - anchor
            gap_y = gap_y + away * away

        @pl.when(t < iters - 1)
        def _():
            for o in range(cols - 1, 0, -1):
                dual_copy(o, True).start()
            for o in range(1, subs):
                forward_copy(o, z, True).start()

            low = lax.broadcasted_iota(jnp.int32, (16, 128), 1) < 64
            gap_line[z] = jnp.where(
                low,
                gap_x + pltpu.roll(gap_x, 64, 1),
                gap_y + pltpu.roll(gap_y, 64, 1),
            )
            for o in range(cols - 1, 0, -1):
                gap_copy(o, True).start()

            for o in range(1, cols):
                dual_copy(o, False).wait_recv()
                for n in range(1, subs):
                    forward_copy(n, along(o), True).start()
            for o in range(cols):
                for n in range(1, subs):
                    forward_copy(n, along(o), False).wait_recv()

            product(dual_all, 1, adjoint_pair)

            for o in range(1, cols):
                gap_copy(o, False).wait_recv()
            gap = gap_line[0]
            for p in range(1, cols):
                gap = gap + gap_line[p]
            gap_group[slot, g] = gap
            for o in range(1, group):
                group_copy(o, slot, True).start()

            for part in range(chunks):
                for u in range(chunk):
                    j = part * chunk + u
                    adjoint_send[j] = sums[last_col_ref[j]].astype(BF)
                for o in range(1, rows):
                    adjoint_copy(o, slot, part, True).start()

            for o in range(1, group):
                group_copy(o, slot, False).wait_recv()
            gap = gap_group[slot, 0]
            for p in range(1, group):
                gap = gap + gap_group[slot, p]
            sum_x = jnp.sum(jnp.where(low, gap, 0.0), axis=1, keepdims=True)
            sum_y = jnp.sum(jnp.where(low, 0.0, gap), axis=1, keepdims=True)
            sum_x = jnp.broadcast_to(sum_x, (16, 128))
            sum_y = jnp.broadcast_to(sum_y, (16, 128))
            ratio = jnp.sqrt((sum_y / total_rows + tiny) / (sum_x / total_cols + tiny))
            fresh = jnp.where(restart, jnp.sqrt(weight * ratio), weight)
            weight_ref[...] = fresh
            stride = step_scale / fresh

            for part in range(chunks):
                for o in range(1, rows):
                    adjoint_copy(o, slot, part, False).wait_recv()
                for u in range(chunk):
                    j = part * chunk + u
                    q, n = j // own_cb, j % own_cb
                    gradient = sums[last_col_ref[j]]
                    for o in range(1, rows):
                        gradient = gradient + adjoint_recv[slot, across(o), j].astype(F32)
                    old = primal[j]
                    new = old - stride * (bounds[q, 0, n : n + 1, :] - gradient)
                    new = jnp.maximum(new, bounds[q, 1, n : n + 1, :])
                    new = jnp.minimum(new, bounds[q, 2, n : n + 1, :])
                    primal_new[j] = new
                    bar[j] = (2.0 * new - old).astype(BF)

            for o in range(1, cols):
                dual_copy(o, True).wait_send()
                gap_copy(o, True).wait_send()
            for o in range(1, subs):
                for q in order:
                    forward_copy(o, q, True).wait_send()
            for o in range(1, group):
                group_copy(o, slot, True).wait_send()
            for o in range(1, rows):
                for part in range(chunks):
                    adjoint_copy(o, slot, part, True).wait_send()

        for o in range(1, cols):
            image_copy(o, True).wait_send()
        for o in range(1, subs):
            for q in order:
                pair_copy(o, q, True).wait_send()
        return jnp.where(restart, 0.0, count)

    lax.fori_loop(0, iters, iteration, jnp.zeros((), F32))
    for i in range(own_cb):
        primal_out[:, i * 128 : (i + 1) * 128] = primal[r * own_cb + i]
    for i in range(own_rb):
        dual_out[:, i * 128 : (i + 1) * 128] = dual[i]


def shards(
    rows,
    cols,
    subs,
    a_blocks,
    block_rows,
    block_cols,
    block_count,
    cost,
    lower,
    span,
    bound_kind,
    demand,
    restart_flags,
):
    blocks = a_blocks[0, 0]
    slots = blocks.shape[0]
    peers = cols * subs
    own_rb = demand.shape[1] // 128
    own_cb = cost.shape[0] // 128
    row_blocks = own_rb * peers
    col_blocks = own_cb * rows
    iters = restart_flags.shape[0]
    unroll = 96
    chunk = own_cb // 2
    live = jnp.arange(slots) < block_count[0, 0]
    row_list = block_rows[0, 0]
    col_list = block_cols[0, 0]
    slot_f, source_f, same_f, last_row = order_slots(
        row_list, col_list, live, row_blocks, col_blocks
    )
    slot_a, source_a, same_a, last_col = order_slots(
        col_list, row_list, live, col_blocks, row_blocks
    )
    index = jnp.stack([slot_f, source_f, slot_a, source_a])
    same = jnp.stack([same_f, same_a])
    sizes = (rows, cols, subs, iters, slots, own_rb, own_cb, unroll, chunk)
    smem = pl.BlockSpec(memory_space=pltpu.SMEM)
    vmem = pl.BlockSpec(memory_space=pltpu.VMEM)
    dma = pltpu.SemaphoreType.DMA
    tile = (16, 128)
    call = pl.pallas_call(
        functools.partial(kernel, sizes),
        out_shape=(
            jax.ShapeDtypeStruct((16, own_cb * 128), F32),
            jax.ShapeDtypeStruct((16, own_rb * 128), F32),
        ),
        in_specs=[smem] * 5 + [pl.BlockSpec(memory_space=pl.ANY)] * 6,
        out_specs=(vmem, vmem),
        scratch_shapes=[
            pltpu.VMEM((slots, 128, 128), BF),
            pltpu.VMEM((slots, 128, 128), BF),
            pltpu.VMEM((3, own_cb, 128), F32),
            pltpu.VMEM((own_cb, 128), jnp.int32),
            pltpu.VMEM((16, own_rb * 128), F32),
            pltpu.VMEM((slots + 1,) + tile, F32),
            pltpu.VMEM((col_blocks + 1,) + tile, BF),
            pltpu.VMEM((row_blocks + 1,) + tile, BF),
            pltpu.VMEM((rows, 3, own_cb, 128), F32),
            pltpu.VMEM((col_blocks,) + tile, F32),
            pltpu.VMEM((col_blocks,) + tile, F32),
            pltpu.VMEM((col_blocks,) + tile, F32),
            pltpu.VMEM((col_blocks,) + tile, F32),
            pltpu.VMEM((own_rb,) + tile, F32),
            pltpu.VMEM((own_rb,) + tile, F32),
            pltpu.VMEM((own_rb,) + tile, F32),
            pltpu.VMEM((subs, cols, own_rb) + tile, F32),
            pltpu.VMEM((subs, cols, own_rb) + tile, F32),
            pltpu.VMEM((cols, own_rb) + tile, BF),
            pltpu.VMEM((cols, own_rb) + tile, BF),
            pltpu.VMEM((col_blocks,) + tile, BF),
            pltpu.VMEM((2, rows, col_blocks) + tile, BF),
            pltpu.VMEM((cols,) + tile, F32),
            pltpu.VMEM((2, rows * subs) + tile, F32),
            pltpu.VMEM(tile, F32),
            dma((6,)),
            dma((2, rows)),
            dma((2, subs, cols)),
            dma((2, cols)),
            dma((2, cols)),
            dma((2, subs, cols)),
            dma((2, cols)),
            dma((2, 2, rows * subs)),
            dma((2, 2, rows, col_blocks // chunk)),
        ],
        compiler_params=pltpu.CompilerParams(
            collective_id=0,
            has_side_effects=True,
            vmem_limit_bytes=60 * 1024 * 1024,
        ),
    )
    as_blocks = lambda v: v.reshape(own_cb, 128)
    return call(
        index,
        same,
        last_row,
        last_col,
        restart_flags,
        blocks,
        as_blocks(cost),
        as_blocks(lower),
        as_blocks(span),
        as_blocks(bound_kind),
        demand,
    )


def solution(mesh):
    placed = (
        P(("inst", "row"), ("col", "sub"), None, None, None),
        P(("inst", "row"), ("col", "sub"), None),
        P(("inst", "row"), ("col", "sub"), None),
        P(("inst", "row"), ("col", "sub")),
        P(("inst", "row", "col", "sub")),
        P(("inst", "row", "col", "sub")),
        P(("inst", "row", "col", "sub")),
        P(("inst", "row", "col", "sub")),
        P(None, ("inst", "row", "col", "sub")),
        P(),
    )
    shape = mesh.shape
    return jax.shard_map(
        functools.partial(shards, shape["row"], shape["col"], shape["sub"]),
        mesh=mesh,
        in_specs=placed,
        out_specs=(P(None, ("inst", "row", "col", "sub")), P(None, ("inst", "row", "col", "sub"))),
        check_vma=False,
    )
```

time: 179 us -> 139 us (0.78)
  Pallas kernels: 168 us -> 131 us
  local copies, waits for them, and re-layouts: 8.25 us -> 2.94 us
  other arithmetic: 1.86 us -> 4.12 us
    pallas_call x1, Pallas kernels: 168 us -> 131 us  [shards(): call(index, same, last_row, last_col, restart_flags, blocks, as_blocks(co...]
    unnamed x16 -> x2, local copies, waits for them, and re-layouts: 8.25 us -> 2.94 us
where the time goes in v2:
time: 139 us
  Pallas kernels  131 us (94%)
  other arithmetic  4.12 us (3%)
  local copies, waits for them, and re-layouts  2.94 us (2%)
    pallas_call x1, Pallas kernels, shards(): call(index, same, last_row, last_col, restart_flags, blocks, as_blocks(co...  131 us
    unnamed x2, local copies, waits for them, and re-layouts  2.94 us

profile of v2, /device:TPU:0, one launch (start us, length us, event | category | flops | bytes accessed | tf_op | source)
XLA Modules:
  0.0 139.2 jit_solution(8815887696120543066)
XLA Ops:
  1.3 0.7 fusion.6
  2.0 0.2 convert_reduce_fusion
  2.2 0.2 convert_reduce_fusion.1
  2.4 0.1 convert_reduce_fusion.2
  2.5 0.5 compare_select_fusion.last_col_ref
  3.0 0.1 convert_reduce_fusion.4
  3.1 0.6 compare_select_fusion.1.last_row_ref
  3.7 0.3 select_reduce_fusion.1
  4.1 0.6 pad_add_fusion.index_ref
  4.7 0.1 fusion.5
  4.7 0.1 fusion.4
  4.8 0.6 add_convert_fusion.same_ref
  5.4 130.8 %shard_map.113 = (f32[16,2048]{1,0:T(8,128)}, f32[16,512]{1,0:T(8,128)}) custom-call(s32[4,192]{1,0:T(4,128)} %pad_add_fusion.index_ref, f32[2,192]{1,0:T(2,128)} %add_convert_fusion.same_ref, s32[32]{0:T(128)} %compare_select_fusion.1.last_row_ref, s32[32]{0:T(128)} %compare_select_fusion.last_col_ref, s32[8]{0:T(128)} %flags_ref.1, ...), custom_call_target="tpu_custom_call" | custom-call | tf_op jit(solution)/shard_map/pallas_call | solution.py:572
  136.3 1.6 %copy.15 = f32[16,2048]{1,0:T(8,128)} copy(f32[16,2048]{1,0:T(8,128)} %get-tuple-element.16) | data formatting | bytes 262144
  137.8 1.4 copy.16

commit v3 on v2

--- a/solution.py
+++ b/solution.py
@@ -81,7 +81,6 @@
     pair_sems,
     image_sems,
     dual_sems,
-    forward_sems,
     gap_sems,
     group_sems,
     adjoint_sems,
@@ -135,7 +134,15 @@
         pl.semaphore_signal(barrier, inc=1, device_id={"col": along(o)}, device_id_type=MESH)
     for o in range(1, group):
         pl.semaphore_signal(barrier, inc=1, device_id=around(o)[1], device_id_type=MESH)
-    pl.semaphore_wait(barrier, cols + group - 2)
+    for o in range(1, cols):
+        for n in range(1, subs):
+            pl.semaphore_signal(
+                barrier,
+                inc=1,
+                device_id={"col": along(o), "sub": beside(n)},
+                device_id_type=MESH,
+            )
+    pl.semaphore_wait(barrier, cols + group - 2 + (cols - 1) * (subs - 1))
 
     def push(src, dst, send_sem, recv_sem, device):
         return pltpu.make_async_remote_copy(
@@ -179,23 +186,18 @@
     def dual_part(q, n):
         return dual_all.at[pl.ds((q * subs + n) * own_rb, own_rb)]
 
-    def dual_copy(o, mine):
-        p = along(o)
-        n = z if mine else p
-        return push(
-            dual_part(z, s), dual_part(n, s), dual_sems.at[0, p], dual_sems.at[1, n], {"col": p}
-        )
-
-    def forward_copy(o, q, mine):
-        p = beside(o)
-        n = s if mine else p
-        return push(
-            dual_part(q, s),
-            dual_part(q, n),
-            forward_sems.at[0, p, q],
-            forward_sems.at[1, n, q],
-            {"sub": p},
-        )
+    def dual_copy(o, n, mine):
+        p, m = along(o), beside(n)
+        source = (z, s) if mine else (p, m)
+        return push(
+            dual_part(z, s),
+            dual_part(*source),
+            dual_sems.at[0, p, m],
+            dual_sems.at[(1,) + source],
+            {"col": p, "sub": m},
+        )
+
+    others = [(o, n) for o in range(cols - 1, -1, -1) for n in range(subs) if o or n]
 
     def gap_copy(o, mine):
         p = along(o)
@@ -381,10 +383,8 @@
 
         @pl.when(t < iters - 1)
         def _():
-            for o in range(cols - 1, 0, -1):
-                dual_copy(o, True).start()
-            for o in range(1, subs):
-                forward_copy(o, z, True).start()
+            for o, n in others:
+                dual_copy(o, n, True).start()
 
             low = lax.broadcasted_iota(jnp.int32, (16, 128), 1) < 64
             gap_line[z] = jnp.where(
@@ -395,13 +395,8 @@
             for o in range(cols - 1, 0, -1):
                 gap_copy(o, True).start()
 
-            for o in range(1, cols):
-                dual_copy(o, False).wait_recv()
-                for n in range(1, subs):
-                    forward_copy(n, along(o), True).start()
-            for o in range(cols):
-                for n in range(1, subs):
-                    forward_copy(n, along(o), False).wait_recv()
+            for o, n in others:
+                dual_copy(o, n, False).wait_recv()
 
             product(dual_all, 1, adjoint_pair)
 
@@ -452,11 +447,9 @@
                     bar[j] = (2.0 * new - old).astype(BF)
 
             for o in range(1, cols):
-                dual_copy(o, True).wait_send()
                 gap_copy(o, True).wait_send()
-            for o in range(1, subs):
-                for q in order:
-                    forward_copy(o, q, True).wait_send()
+            for o, n in others:
+                dual_copy(o, n, True).wait_send()
             for o in range(1, group):
                 group_copy(o, slot, True).wait_send()
             for o in range(1, rows):
@@ -556,8 +549,7 @@
             dma((2, rows)),
             dma((2, subs, cols)),
             dma((2, cols)),
-            dma((2, cols)),
-            dma((2, subs, cols)),
+            dma((2, cols, subs)),
             dma((2, cols)),
             dma((2, 2, rows * subs)),
             dma((2, 2, rows, col_blocks // chunk)),

time: 139 us -> 146 us (1.050)
  Pallas kernels: 131 us -> 138 us
    pallas_call x1, Pallas kernels: 131 us -> 138 us  [shards(): call(index, same, last_row, last_col, restart_flags, blocks, as_blocks(co...]
where the time goes in v3:
time: 146 us
  Pallas kernels  138 us (95%)
  other arithmetic  4.12 us (3%)
  local copies, waits for them, and re-layouts  2.94 us (2%)
    pallas_call x1, Pallas kernels, shards(): call(index, same, last_row, last_col, restart_flags, blocks, as_blocks(co...  138 us
    unnamed x2, local copies, waits for them, and re-layouts  2.94 us

profile of v3, /device:TPU:0, one launch (start us, length us, event | category | flops | bytes accessed | tf_op | source)
XLA Modules:
  0.0 145.9 jit_solution(11553143153742287025)
XLA Ops:
  1.3 0.7 fusion.6
  2.0 0.2 convert_reduce_fusion
  2.2 0.2 convert_reduce_fusion.1
  2.4 0.1 convert_reduce_fusion.2
  2.5 0.5 compare_select_fusion.last_col_ref
  3.0 0.1 convert_reduce_fusion.4
  3.1 0.6 compare_select_fusion.1.last_row_ref
  3.7 0.3 select_reduce_fusion.1
  4.1 0.6 pad_add_fusion.index_ref
  4.7 0.1 fusion.5
  4.7 0.1 fusion.4
  4.8 0.6 add_convert_fusion.same_ref
  5.4 137.5 %shard_map.113 = (f32[16,2048]{1,0:T(8,128)}, f32[16,512]{1,0:T(8,128)}) custom-call(s32[4,192]{1,0:T(4,128)} %pad_add_fusion.index_ref, f32[2,192]{1,0:T(2,128)} %add_convert_fusion.same_ref, s32[32]{0:T(128)} %compare_select_fusion.1.last_row_ref, s32[32]{0:T(128)} %compare_select_fusion.last_col_ref, s32[8]{0:T(128)} %flags_ref.1, ...), custom_call_target="tpu_custom_call" | custom-call | tf_op jit(solution)/shard_map/pallas_call | solution.py:564
  142.9 1.6 %copy.15 = f32[16,2048]{1,0:T(8,128)} copy(f32[16,2048]{1,0:T(8,128)} %get-tuple-element.16) | data formatting | bytes 262144
  144.5 1.4 copy.16

commit v4 on v2

--- a/solution.py
+++ b/solution.py
@@ -500,7 +500,7 @@
     row_blocks = own_rb * peers
     col_blocks = own_cb * rows
     iters = restart_flags.shape[0]
-    unroll = 96
+    unroll = slots
     chunk = own_cb // 2
     live = jnp.arange(slots) < block_count[0, 0]
     row_list = block_rows[0, 0]

time: 139 us -> 136 us (0.978)
  Pallas kernels: 131 us -> 127 us
    pallas_call x1, Pallas kernels: 131 us -> 127 us  [shards(): call(index, same, last_row, last_col, restart_flags, blocks, as_blocks(co...]
where the time goes in v4:
time: 136 us
  Pallas kernels  127 us (93%)
  other arithmetic  4.12 us (3%)
  local copies, waits for them, and re-layouts  2.94 us (2%)
    pallas_call x1, Pallas kernels, shards(): call(index, same, last_row, last_col, restart_flags, blocks, as_blocks(co...  127 us
    unnamed x2, local copies, waits for them, and re-layouts  2.94 us

profile of v4, /device:TPU:0, one launch (start us, length us, event | category | flops | bytes accessed | tf_op | source)
XLA Modules:
  0.0 135.9 jit_solution(16075637576961695239)
XLA Ops:
  1.3 0.7 fusion.6
  2.0 0.2 convert_reduce_fusion
  2.2 0.2 convert_reduce_fusion.1
  2.4 0.1 convert_reduce_fusion.2
  2.5 0.5 compare_select_fusion.last_col_ref
  3.0 0.1 convert_reduce_fusion.4
  3.1 0.6 compare_select_fusion.1.last_row_ref
  3.7 0.3 select_reduce_fusion.1
  4.1 0.6 pad_add_fusion.index_ref
  4.7 0.1 fusion.5
  4.7 0.1 fusion.4
  4.8 0.6 add_convert_fusion.same_ref
  5.4 127.5 %shard_map.113 = (f32[16,2048]{1,0:T(8,128)}, f32[16,512]{1,0:T(8,128)}) custom-call(s32[4,192]{1,0:T(4,128)} %pad_add_fusion.index_ref, f32[2,192]{1,0:T(2,128)} %add_convert_fusion.same_ref, s32[32]{0:T(128)} %compare_select_fusion.1.last_row_ref, s32[32]{0:T(128)} %compare_select_fusion.last_col_ref, s32[8]{0:T(128)} %flags_ref.1, ...), custom_call_target="tpu_custom_call" | custom-call | tf_op jit(solution)/shard_map/pallas_call | solution.py:572
  132.9 1.6 %copy.15 = f32[16,2048]{1,0:T(8,128)} copy(f32[16,2048]{1,0:T(8,128)} %get-tuple-element.16) | data formatting | bytes 262144
  134.5 1.4 %copy.16 = f32[16,512]{1,0:T(8,128)} copy(f32[16,512]{1,0:T(8,128)} %get-tuple-element.17) | data formatting | bytes 65536
